TPU v7x, 32 devices: a whole 2x2x4 slice. The times are simulated.
32 devices in a mesh: req: 8 (over z, y), kvh: 4 (over x, core).
Axes of the slice: x: 2, y: 2, z: 4, core: 2. Of those that a mesh axis runs over, the one named last changes fastest.
Arguments:
- queries: bfloat16 [512, 4, 8, 128], P('req', 'kvh')
- key_cache: bfloat16 [1280, 4, 128, 128], P('req', 'kvh')
- value_cache: bfloat16 [1280, 4, 128, 128], P('req', 'kvh'), may hold values from -24 to 24
- lengths: int32 [512], P('req'), may hold values from 1 to 4096, as said below
- page_table: int32 [512, 32], P('req'), may hold values from 0 to 159, as said below
- residual_in: bfloat16 [512, 2048], P(('req', 'kvh')), may hold values from -4 to 4
- w_out: bfloat16 [4096, 2048], P('kvh'), may hold values from -0.09375 to 0.09375
- norm_gain: bfloat16 [2048], replicated, may hold values from 0.099609375 to 1.8984375
- route_logits: float32 [512, 8], P(('req', 'kvh'))
- routes: int32 [512, 8], P(('req', 'kvh')), may hold values from 0 to 31, as said below
- w_gate: bfloat16 [32, 2048, 768], P(('req', 'kvh')), may hold values from -0.125 to 0.125
- w_up: bfloat16 [32, 2048, 768], P(('req', 'kvh')), may hold values from -0.125 to 0.125
- w_down: bfloat16 [32, 768, 2048], P(('req', 'kvh')), may hold values from -0.21875 to 0.21875
Outputs:
- layer_out: bfloat16 [512, 2048], P(('req', 'kvh'))
Inputs may be any that keep to these rules, and one draw needn't show every extreme that they name: `lengths`: every request of a block of 64 has between 1 and 32 pages; some request reaches 4096. `page_table`: local page numbers within the pool of the request's block of 64 requests. Entries 0 to ceil(lengths / 128) - 1 of the requests of one block are all distinct; later entries repeat the request's last used page. `routes`: each token names 8 different experts. Of the 16 tokens of one device, at most 8 name the same expert, and some expert is named by exactly 8 tokens of every device.
All inputs are finite; a program needn't handle non-finite values.
Results may differ from a plain program's by a relative error of at most 0.0054.
Values may be sent and summed in bfloat16 or wider, within the bound.
A program may use at most 192 MiB of HBM per device.

v0:
```python
import jax
import jax.numpy as jnp
from jax import lax
from jax.sharding import PartitionSpec as P


def swish_gate(gate_part, up_part):
    return gate_part / (1.0 + jnp.exp(-gate_part)) * up_part


def usable_slots(lengths, page_table, pool_pages, page_slots):
    entry_count = page_table.shape[1]
    used_pages = (lengths + page_slots - 1) // page_slots
    columns = jnp.arange(entry_count, dtype=jnp.int32)
    pool_ids = jnp.arange(pool_pages, dtype=jnp.int32)
    matched = (page_table[:, :, None] == pool_ids[None, None, :]) & (
        columns[None, :, None] < used_pages[:, None, None]
    )
    owned_page = jnp.any(matched, axis=1)
    first_pos = jnp.sum(jnp.where(matched, columns[None, :, None] * page_slots, 0), axis=1)
    offsets = jnp.arange(page_slots, dtype=jnp.int32)
    position = first_pos[:, :, None] + offsets[None, None, :]
    usable = owned_page[:, :, None] & (position < lengths[:, None, None])
    return usable.reshape(lengths.shape[0], pool_pages * page_slots)


def earlier_count(pair_routes):
    positions = jnp.arange(pair_routes.shape[0], dtype=jnp.int32)
    same_expert = pair_routes[:, None] == pair_routes[None, :]
    before = positions[None, :] < positions[:, None]
    return jnp.sum(same_expert & before, axis=1)


def local(
    queries,
    key_cache,
    value_cache,
    lengths,
    page_table,
    residual_in,
    w_out,
    norm_gain,
    route_logits,
    routes,
    w_gate,
    w_up,
    w_down,
):
    req_count, single_head, group_count, head_dim = queries.shape
    pool_pages, single_kv, page_slots, key_dim = key_cache.shape
    usable = usable_slots(lengths, page_table, pool_pages, page_slots)
    query_rows = queries.reshape(req_count * group_count, head_dim)
    key_rows = key_cache.reshape(pool_pages * page_slots, head_dim)
    value_rows = value_cache.reshape(pool_pages * page_slots, head_dim)
    scores = jnp.einsum(
        "qd,kd->qk", query_rows, key_rows, preferred_element_type=jnp.float32
    ) * head_dim ** (-0.5)
    scores = scores.reshape(req_count, group_count, pool_pages * page_slots)
    key_mask = usable[:, None, :]
    row_max = jnp.max(jnp.where(key_mask, scores, -jnp.inf), axis=-1, keepdims=True)
    weights = jnp.where(key_mask, jnp.exp(scores - row_max), 0.0)
    denominator = jnp.sum(weights, axis=-1, keepdims=True)
    rounded = weights.astype(jnp.bfloat16).reshape(req_count * group_count, pool_pages * page_slots)
    mixed_values = jnp.dot(rounded, value_rows, preferred_element_type=jnp.float32).reshape(
        req_count, group_count, head_dim
    )
    attended = (
        (mixed_values / denominator).astype(jnp.bfloat16).reshape(req_count, group_count * head_dim)
    )
    stream = residual_in.astype(jnp.float32) + lax.psum_scatter(
        jnp.dot(attended, w_out, preferred_element_type=jnp.float32),
        "kvh",
        scatter_dimension=0,
        tiled=True,
    )
    inverse_rms = lax.rsqrt(jnp.mean(stream * stream, axis=-1, keepdims=True) + 1e-06)
    normed = (stream * inverse_rms * norm_gain.astype(jnp.float32)).astype(jnp.bfloat16)
    logit_max = jnp.max(route_logits, axis=-1, keepdims=True)
    logit_exp = jnp.exp(route_logits - logit_max)
    gate_weights = logit_exp / jnp.sum(logit_exp, axis=-1, keepdims=True)
    expert_count = lax.axis_size("req") * lax.axis_size("kvh")
    token_count, pick_count = routes.shape
    model_width = normed.shape[1]
    slot_depth = max(2, 2 * token_count * pick_count // expert_count)
    pair_routes = routes.reshape(token_count * pick_count)
    pair_slots = earlier_count(pair_routes)
    target = pair_routes * slot_depth + pair_slots
    slot_ids = jnp.arange(expert_count * slot_depth, dtype=jnp.int32)
    chosen = (target[None, :] == slot_ids[:, None]).reshape(
        expert_count * slot_depth, token_count, pick_count
    )
    send_matrix = jnp.any(chosen, axis=-1).astype(jnp.bfloat16)
    outgoing = jnp.dot(send_matrix, normed, preferred_element_type=jnp.float32).astype(jnp.bfloat16)
    outgoing = outgoing.reshape(expert_count, slot_depth, model_width)
    arrived = lax.all_to_all(outgoing, ("req", "kvh"), split_axis=0, concat_axis=0, tiled=True)
    sources, width_slots, arrived_width = arrived.shape
    flat_rows = arrived.reshape(sources * width_slots, arrived_width)
    gate_part = jnp.dot(flat_rows, w_gate[0], preferred_element_type=jnp.float32)
    up_part = jnp.dot(flat_rows, w_up[0], preferred_element_type=jnp.float32)
    hidden = swish_gate(gate_part, up_part).astype(jnp.bfloat16)
    produced = jnp.dot(hidden, w_down[0], preferred_element_type=jnp.float32).astype(jnp.bfloat16)
    returned = lax.all_to_all(
        produced.reshape(sources, width_slots, arrived_width),
        ("req", "kvh"),
        split_axis=0,
        concat_axis=0,
        tiled=True,
    )
    returned = returned.reshape(expert_count * slot_depth, model_width)
    pick_matrix = (target[:, None] == slot_ids[None, :]).astype(jnp.bfloat16)
    picked = jnp.dot(pick_matrix, returned, preferred_element_type=jnp.float32).reshape(
        token_count, pick_count, model_width
    )
    mixture = jnp.sum(gate_weights[:, :, None] * picked, axis=1)
    return (stream + mixture).astype(jnp.bfloat16)


def solution(mesh):
    in_specs = (
        P("req", "kvh", None, None),
        P("req", "kvh", None, None),
        P("req", "kvh", None, None),
        P("req"),
        P("req", None),
        P(("req", "kvh"), None),
        P("kvh", None),
        P(),
        P(("req", "kvh"), None),
        P(("req", "kvh"), None),
        P(("req", "kvh"), None, None),
        P(("req", "kvh"), None, None),
        P(("req", "kvh"), None, None),
    )
    out_specs = P(("req", "kvh"), None)
    return jax.shard_map(local, mesh=mesh, in_specs=in_specs, out_specs=out_specs, check_vma=False)
```

profile of v0, /device:TPU:0, one launch (start us, length us, event | category | flops | bytes accessed | tf_op | source)
XLA Modules:
  0.0 186.1 jit_solution(5047588856199653318)
XLA Ops:
  6.6 0.9 copy.22
  7.5 0.7 and_select_fusion
  8.2 0.1 iota_compare_fusion.4
  8.3 0.7 fusion.23
  9.0 1.0 select_reduce_fusion
  10.1 1.5 add.62
  11.6 1.9 %and.33 = pred[64,160,128]{2,1,0:T(8,128)(4,1)S(1)} broadcast(pred[64,160]{1,0:T(8,128)(4,1)S(1)} %fusion.23), dimensions={0,1} | broadcast | bytes 1320960 | tf_op jit(solution)/shard_map/and | solution.py:23
  13.5 4.4 %fusion.8 = pred[64,20480]{1,0:T(8,128)(4,1)S(1)} fusion(s32[8,8,160,128]{3,2,1,0:T(8,128)S(1)} %bitcast.90, pred[8,8,160,128]{3,2,1,0:T(8,128)(4,1)S(1)} %bitcast.92, s32[64]{0:T(128)S(1)} %copy-done.9, s32[20480]{0:T(1024)S(1)} %iota_bitcast_fusion), kind=kLoop, calls=%fused_computation.10 | loop fusion | flops 3932160 | bytes 7946496 | tf_op jit(solution)/shard_map/and | solution.py:23
  18.0 18.7 %fusion = (f32[512]{0:T(512)S(1)}, f32[512,20480]{1,0:T(8,128)}) fusion(pred[64,20480]{1,0:T(8,128)(4,1)S(1)} %fusion.8, bf16[20480,128]{1,0:T(8,128)(2,1)} %bitcast.91, bf16[64,1,8,128]{3,2,1,0:T(8,128)(2,1)S(1)} %copy-done.5), kind=kOutput, calls=%fused_computation.2 | convolution fusion | flops 2715811328 | bytes 48629760 | tf_op jit(solution)/shard_map/qd,kd->qk/dot_general | solution.py:55
  36.7 19.6 %fusion.1 = f32[512]{0:T(512)S(1)} fusion(f32[512,20480]{1,0:T(8,128)} %get-tuple-element.6, f32[512]{0:T(512)S(1)} %get-tuple-element.5, pred[64,20480]{1,0:T(8,128)(4,1)S(1)} %fusion.8), kind=kLoop, calls=%fused_computation.3 | loop fusion | flops 41942528 | bytes 43257856 | tf_op jit(solution)/shard_map/reduce_sum | solution.py:62
  56.3 0.1 div.40
  56.4 18.6 %fusion.37 = bf16[64,8,128]{2,1,0:T(8,128)(2,1)S(1)} fusion(bf16[20480,128,1]{1,0,2:T(8,128)(2,1)} %bitcast.94, f32[512,20480]{1,0:T(8,128)} %get-tuple-element.6, f32[512]{0:T(512)S(1)} %get-tuple-element.5, pred[64,20480]{1,0:T(8,128)(4,1)} %copy-done.1, f32[64,8]{1,0:T(8,128)S(1)} %div.40), kind=kOutput, calls=%fused_computation.33 | convolution fusion | flops 2726428672 | bytes 48631808 | tf_op jit(solution)/shard_map/dot_general | solution.py:64
  75.1 3.9 %fusion.45 = f32[64,2048]{1,0:T(8,128)} fusion(bf16[1024,2048]{1,0:T(8,128)(2,1)} %param.19, bf16[8,8,8,128]{3,2,1,0:T(8,128)(2,1)S(1)} %bitcast.93), kind=kOutput, calls=%fused_computation.35 | convolution fusion | flops 268435456 | bytes 4849664 | tf_op jit(solution)/shard_map/dot_general | solution.py:71
  78.9 0.0 reduce-scatter.2.cloned.1.call-update
  79.0 0.1 copy.24
  79.0 0.1 eq.74
  79.1 0.2 convert_reduce_fusion
  79.3 0.1 reduce_sum.60
  79.4 0.0 copy-done.8
  79.4 0.1 fusion.52
  79.5 23.9 %reduce-scatter.2.cloned.1.call-done = f32[16,2048]{1,0:T(8,128)} async-done(((f32[64,2048]{1,0:T(8,128)}), f32[16,2048]{1,0:T(8,128)}) %reduce-scatter.2.cloned.1.call-update) | async-done | bytes 131088 | tf_op jit(solution)/shard_map/reduce_scatter | solution.py:70
  103.5 1.0 multiply_reduce_fusion
  104.5 1.4 fusion.21
  105.9 30.6 %all_to_all.10 = bf16[32,8,2048]{2,1,0:T(8,128)(2,1)S(1)} all-to-all(bf16[32,8,2048]{2,1,0:T(8,128)(2,1)S(1)} %fusion.21), channel_id=1, replica_groups=mesh['req'=8,'kvh'=4] {'req','kvh'}, dimensions={0} | all-to-all | bytes 2097152 | tf_op jit(solution)/shard_map/all_to_all | solution.py:95
  136.6 1.0 copy-done.3
  137.6 3.8 %fusion.13 = f32[256,768]{1,0:T(8,128)} fusion(bf16[1,2048,768]{2,1,0:T(8,128)(2,1)} %param.23, bf16[32,8,2048]{2,1,0:T(8,128)(2,1)S(1)} %all_to_all.10), kind=kOutput, calls=%fused_computation.15 | convolution fusion | flops 805306368 | bytes 4980736 | tf_op jit(solution)/shard_map/dot_general | solution.py:98
  141.4 5.5 %fusion.18 = bf16[32,8,2048]{2,1,0:T(8,128)(2,1)} fusion(bf16[1,768,2048]{2,1,0:T(8,128)(2,1)S(1)} %copy-done, bf16[1,2048,768]{2,1,0:T(8,128)(2,1)} %param.24, bf16[32,8,2048]{2,1,0:T(8,128)(2,1)} %copy-done.3, f32[256,768]{1,0:T(8,128)} %fusion.13), kind=kOutput, calls=%fused_computation.19 | convolution fusion | flops 1612120064 | bytes 9175040 | tf_op jit(solution)/shard_map/dot_general | solution.py:101
  146.9 3.7 %all-to-all-start.1 = ((bf16[32,8,2048]{2,1,0:T(8,128)(2,1)}), bf16[32,8,2048]{2,1,0:T(8,128)(2,1)}, u32[]{:S(2)}, u32[]{:S(2)}) async-start(bf16[32,8,2048]{2,1,0:T(8,128)(2,1)} %fusion.18), calls=%async_computation.2 | async-start | bytes 2097152 | tf_op jit(solution)/shard_map/all_to_all | solution.py:102
  150.8 0.1 copy.23
  150.8 26.1 %all-to-all-done.1 = bf16[32,8,2048]{2,1,0:T(8,128)(2,1)} async-done(((bf16[32,8,2048]{2,1,0:T(8,128)(2,1)}), bf16[32,8,2048]{2,1,0:T(8,128)(2,1)}, u32[]{:S(2)}, u32[]{:S(2)}) %all-to-all-start.1) | async-done | bytes 1048608 | tf_op jit(solution)/shard_map/all_to_all | solution.py:102
  176.9 1.7 fusion.30
  178.6 0.6 add_convert_fusion
  (27 shorter events, 0.1 us)
Async XLA Ops:
  6.5 134.8 %copy-start = (bf16[1,768,2048]{2,1,0:T(8,128)(2,1)S(1)}, bf16[1,768,2048]{2,1,0:T(8,128)(2,1)}, u32[]{:S(2)}) copy-start(bf16[1,768,2048]{2,1,0:T(8,128)(2,1)} %param.25) | copy-start | bytes 9437188
  6.5 7.0 %copy-start.9 = (s32[64]{0:T(128)S(1)}, s32[64]{0:T(128)}, u32[]{:S(2)}) copy-start(s32[64]{0:T(128)} %param.16) | copy-start | bytes 772
  6.5 97.0 %reduce-scatter.2.cloned.1.call-start = ((), (), s32[]{:S(2)}) async-start(), calls=%async_computation.3 | async-start | bytes 655360 | tf_op jit(solution)/shard_map/reduce_scatter | solution.py:70
  11.6 6.4 %copy-start.5 = (bf16[64,1,8,128]{3,2,1,0:T(8,128)(2,1)S(1)}, bf16[64,1,8,128]{3,2,1,0:T(8,128)(2,1)}, u32[]{:S(2)}) copy-start(bf16[64,1,8,128]{3,2,1,0:T(8,128)(2,1)} %param.13) | copy-start | bytes 393220
  17.9 18.7 %copy-start.1 = (pred[64,20480]{1,0:T(8,128)(4,1)}, pred[64,20480]{1,0:T(8,128)(4,1)S(1)}, u32[]{:S(2)}) copy-start(pred[64,20480]{1,0:T(8,128)(4,1)S(1)} %fusion.8) | copy-start | bytes 3932164
  75.0 3.9 %copy-start.7 = (s32[16,8]{0,1:T(8,128)S(1)}, s32[16,8]{0,1:T(8,128)}, u32[]{:S(2)}) copy-start(s32[16,8]{0,1:T(8,128)} %param.22) | copy-start | bytes 1540
  75.0 4.4 %copy-start.8 = (bf16[2048]{0:T(1024)(128)(2,1)S(1)}, bf16[2048]{0:T(1024)(128)(2,1)}, u32[]{:S(2)}) copy-start(bf16[2048]{0:T(1024)(128)(2,1)} %param.20) | copy-start | bytes 12292
  75.1 28.4 %copy-start.4 = (bf16[16,2048]{1,0:T(8,128)(2,1)S(1)}, bf16[16,2048]{1,0:T(8,128)(2,1)}, u32[]{:S(2)}) copy-start(bf16[16,2048]{1,0:T(8,128)(2,1)} %param.18) | copy-start | bytes 196612
  136.6 1.0 copy-start.3
  141.4 9.3 %copy-start.6 = (f32[16,8]{0,1:T(8,128)S(1)}, f32[16,8]{0,1:T(8,128)}, u32[]{:S(2)}) copy-start(f32[16,8]{0,1:T(8,128)} %param.21) | copy-start | bytes 1540
  141.4 37.2 %copy-start.2 = (f32[16,2048]{1,0:T(8,128)S(1)}, f32[16,2048]{1,0:T(8,128)}, u32[]{:S(2)}) copy-start(f32[16,2048]{1,0:T(8,128)} %reduce-scatter.2.cloned.1.call-done) | copy-start | bytes 393220
  146.9 30.0 %all-to-all-start.1 = ((bf16[32,8,2048]{2,1,0:T(8,128)(2,1)}), bf16[32,8,2048]{2,1,0:T(8,128)(2,1)}, u32[]{:S(2)}, u32[]{:S(2)}) async-start(bf16[32,8,2048]{2,1,0:T(8,128)(2,1)} %fusion.18), calls=%async_computation.2 | async-start | bytes 2097152 | tf_op jit(solution)/shard_map/all_to_all | solution.py:102
Sparse Core Ops, SparseCore 0:
  79.1 24.3 reduce-scatter.1
where the time goes:
time: 187 us; the launch traced here: 186 us
  matrix products  53.6 us (29%)
  waiting for transfers between devices  50 us (27%)
  blocking collectives  30.6 us (16%)
  other arithmetic  28.6 us (15%)
  between operations  13.6 us (7%)
  local copies, waits for them, and re-layouts  5.9 us (3%)
  starting transfers between devices  3.75 us (2%)
    all_to_all x1, blocking collectives, local(): lax.all_to_all(outgoing, ('req', 'kvh'), split_axis=0, concat_axis=0, til...  30.6 us
    all_to_all x1, waiting for transfers between devices, local(): lax.all_to_all(produced.reshape(sources, width_slots, arrived_width), ('r...  26.1 us
    reduce_scatter x1, waiting for transfers between devices, local(): lax.psum_scatter(jnp.dot(attended, w_out, preferred_element_type=jnp.floa...  23.9 us
    reduce_sum x1, other arithmetic, local(): denominator = jnp.sum(weights, axis=-1, keepdims=True)  19.6 us
    dot_general x1, matrix products, local(): jnp.einsum('qd,kd->qk', query_rows, key_rows, preferred_element_type=jnp....  18.7 us
    dot_general x1, matrix products, local(): jnp.dot(rounded, value_rows, preferred_element_type=jnp.float32)  18.6 us
    dot_general x1, matrix products, local(): jnp.dot(hidden, w_down[0], preferred_element_type=jnp.float32)  5.55 us
    and x1, other arithmetic, usable_slots(): usable = owned_page[:, :, None] & (position < lengths[:, None, None])  4.39 us
  transfers between devices with their start and end apart: 2, of which 2 were waited for; matrix products, arithmetic and copies ran while one was open for 0% of the time, Pallas kernels for 0%

commit v1 on v0

--- a/solution.py
+++ b/solution.py
@@ -1,27 +1,157 @@
+import functools
+
 import jax
 import jax.numpy as jnp
 from jax import lax
+from jax.experimental import pallas as pl
+from jax.experimental.pallas import tpu as pltpu
 from jax.sharding import PartitionSpec as P
+
+MESH = pl.DeviceIdType.MESH
 
 
 def swish_gate(gate_part, up_part):
     return gate_part / (1.0 + jnp.exp(-gate_part)) * up_part
 
 
-def usable_slots(lengths, page_table, pool_pages, page_slots):
+def page_owners(lengths, page_table, pool_pages, page_slots):
     entry_count = page_table.shape[1]
-    used_pages = (lengths + page_slots - 1) // page_slots
     columns = jnp.arange(entry_count, dtype=jnp.int32)
     pool_ids = jnp.arange(pool_pages, dtype=jnp.int32)
-    matched = (page_table[:, :, None] == pool_ids[None, None, :]) & (
-        columns[None, :, None] < used_pages[:, None, None]
-    )
-    owned_page = jnp.any(matched, axis=1)
-    first_pos = jnp.sum(jnp.where(matched, columns[None, :, None] * page_slots, 0), axis=1)
-    offsets = jnp.arange(page_slots, dtype=jnp.int32)
-    position = first_pos[:, :, None] + offsets[None, None, :]
-    usable = owned_page[:, :, None] & (position < lengths[:, None, None])
-    return usable.reshape(lengths.shape[0], pool_pages * page_slots)
+    room = lengths[:, None] - columns[None, :] * page_slots
+    counts = jnp.clip(room, 0, page_slots)
+    matched = page_table[:, :, None] == pool_ids[None, None, :]
+    fill = jnp.sum(jnp.where(matched, counts[:, :, None], 0), axis=1)
+    return fill > 0, jnp.sum(fill, axis=0)
+
+
+def page_kernel(scale, filled_ref, query_ref, key_ref, value_ref, top_ref, total_ref, mixed_ref):
+    scores = jnp.einsum(
+        "pgd,psd->pgs", query_ref[...], key_ref[...], preferred_element_type=jnp.float32
+    ) * scale
+    slots = lax.broadcasted_iota(jnp.int32, scores.shape, 2)
+    usable = slots < filled_ref[...]
+    top = jnp.max(jnp.where(usable, scores, -jnp.inf), axis=-1, keepdims=True)
+    weights = jnp.where(usable, jnp.exp(scores - top), 0.0)
+    top_ref[...] = jnp.broadcast_to(top, scores.shape)
+    total_ref[...] = jnp.broadcast_to(jnp.sum(weights, axis=-1, keepdims=True), scores.shape)
+    mixed_ref[...] = jnp.einsum(
+        "pgs,psd->pgd",
+        weights.astype(jnp.bfloat16),
+        value_ref[...],
+        preferred_element_type=jnp.float32,
+    )
+
+
+def page_attention(page_queries, keys, values, filled):
+    pool_pages, group_count, head_dim = page_queries.shape
+    page_slots = keys.shape[1]
+    chunk = next(c for c in (32, 16, 8, 4, 2, 1) if pool_pages % c == 0)
+    fills = jnp.broadcast_to(filled[:, None, None], (pool_pages, 1, page_slots))
+    small = pl.BlockSpec((chunk, group_count, page_slots), lambda i: (i, 0, 0))
+    wide = pl.BlockSpec((chunk, group_count, head_dim), lambda i: (i, 0, 0))
+    cache = pl.BlockSpec((chunk, page_slots, head_dim), lambda i: (i, 0, 0))
+    stat = jax.ShapeDtypeStruct((pool_pages, group_count, page_slots), jnp.float32)
+    return pl.pallas_call(
+        functools.partial(page_kernel, head_dim ** (-0.5)),
+        grid=(pool_pages // chunk,),
+        in_specs=[pl.BlockSpec((chunk, 1, page_slots), lambda i: (i, 0, 0)), wide, cache, cache],
+        out_specs=[small, small, wide],
+        out_shape=[stat, stat, jax.ShapeDtypeStruct(page_queries.shape, jnp.float32)],
+        compiler_params=pltpu.CompilerParams(vmem_limit_bytes=24 * 1024 * 1024),
+    )(fills, page_queries, keys, values)
+
+
+def attend(queries, key_cache, value_cache, lengths, page_table):
+    req_count, single_head, group_count, head_dim = queries.shape
+    pool_pages, single_kv, page_slots, key_dim = key_cache.shape
+    owned, filled = page_owners(lengths, page_table, pool_pages, page_slots)
+    spread = owned.astype(jnp.bfloat16)
+    page_queries = jnp.einsum(
+        "rp,rx->px",
+        spread,
+        queries.reshape(req_count, group_count * head_dim),
+        preferred_element_type=jnp.float32,
+    ).astype(jnp.bfloat16)
+    top, total, mixed = page_attention(
+        page_queries.reshape(pool_pages, group_count, head_dim),
+        key_cache.reshape(pool_pages, page_slots, head_dim),
+        value_cache.reshape(pool_pages, page_slots, head_dim),
+        filled,
+    )
+    top, total = top[:, :, 0].T, total[:, :, 0].T
+    row_top = jnp.max(jnp.where(owned[None], top[:, None, :], -jnp.inf), axis=-1)
+    page_top = jnp.sum(jnp.where(owned[None], row_top[:, :, None], 0.0), axis=1)
+    factor = jnp.exp(top - page_top)
+    denominator = jnp.sum(jnp.where(owned[None], (total * factor)[:, None, :], 0.0), axis=-1)
+    scaled = mixed * factor.T[:, :, None]
+    high = scaled.astype(jnp.bfloat16)
+    low = (scaled - high.astype(jnp.float32)).astype(jnp.bfloat16)
+    parts = jnp.concatenate([high, low], axis=0).reshape(2 * pool_pages, group_count * head_dim)
+    gathered = jnp.dot(
+        jnp.concatenate([spread, spread], axis=1), parts, preferred_element_type=jnp.float32
+    ).reshape(req_count, group_count, head_dim)
+    return (gathered / denominator.T[:, :, None]).astype(jnp.bfloat16).reshape(
+        req_count, group_count * head_dim
+    )
+
+
+def sum_kernel(
+    peers, part_ref, residual_ref, gain_ref, stream_ref, normed_ref, outgoing, landed, send_sems, recv_sems
+):
+    me = lax.axis_index("kvh")
+    rows = residual_ref.shape[0]
+    barrier = pltpu.get_barrier_semaphore()
+    for step in range(1, peers):
+        pl.semaphore_signal(
+            barrier, inc=1, device_id={"kvh": lax.rem(me + step, peers)}, device_id_type=MESH
+        )
+    for step in range(1, peers):
+        block = pl.multiple_of(lax.rem(me + step, peers) * rows, rows)
+        outgoing[step - 1] = part_ref[pl.ds(block, rows), :].astype(jnp.bfloat16)
+    pl.semaphore_wait(barrier, peers - 1)
+    copies = []
+    for step in range(1, peers):
+        copy = pltpu.make_async_remote_copy(
+            src_ref=outgoing.at[step - 1],
+            dst_ref=landed.at[step - 1],
+            send_sem=send_sems.at[step - 1],
+            recv_sem=recv_sems.at[step - 1],
+            device_id={"kvh": lax.rem(me + step, peers)},
+            device_id_type=MESH,
+        )
+        copy.start()
+        copies.append(copy)
+    stream = residual_ref[...].astype(jnp.float32) + part_ref[pl.ds(pl.multiple_of(me * rows, rows), rows), :]
+    for step, copy in enumerate(copies):
+        copy.wait()
+        stream = stream + landed[step].astype(jnp.float32)
+    stream_ref[...] = stream
+    inverse_rms = lax.rsqrt(jnp.mean(stream * stream, axis=-1, keepdims=True) + 1e-06)
+    normed_ref[...] = (stream * inverse_rms * gain_ref[...].astype(jnp.float32)).astype(jnp.bfloat16)
+
+
+def summed_stream(part, residual_in, norm_gain, peers):
+    rows, width = residual_in.shape
+    vmem = pl.BlockSpec(memory_space=pltpu.VMEM)
+    return pl.pallas_call(
+        functools.partial(sum_kernel, peers),
+        in_specs=[vmem] * 3,
+        out_specs=[vmem] * 2,
+        out_shape=[
+            jax.ShapeDtypeStruct((rows, width), jnp.float32),
+            jax.ShapeDtypeStruct((rows, width), jnp.bfloat16),
+        ],
+        scratch_shapes=[
+            pltpu.VMEM((peers - 1, rows, width), jnp.bfloat16),
+            pltpu.VMEM((peers - 1, rows, width), jnp.bfloat16),
+            pltpu.SemaphoreType.DMA((peers - 1,)),
+            pltpu.SemaphoreType.DMA((peers - 1,)),
+        ],
+        compiler_params=pltpu.CompilerParams(
+            collective_id=0, has_side_effects=True, vmem_limit_bytes=16 * 1024 * 1024
+        ),
+    )(part, residual_in, norm_gain.reshape(1, width))
 
 
 def earlier_count(pair_routes):
@@ -46,35 +176,9 @@
     w_up,
     w_down,
 ):
-    req_count, single_head, group_count, head_dim = queries.shape
-    pool_pages, single_kv, page_slots, key_dim = key_cache.shape
-    usable = usable_slots(lengths, page_table, pool_pages, page_slots)
-    query_rows = queries.reshape(req_count * group_count, head_dim)
-    key_rows = key_cache.reshape(pool_pages * page_slots, head_dim)
-    value_rows = value_cache.reshape(pool_pages * page_slots, head_dim)
-    scores = jnp.einsum(
-        "qd,kd->qk", query_rows, key_rows, preferred_element_type=jnp.float32
-    ) * head_dim ** (-0.5)
-    scores = scores.reshape(req_count, group_count, pool_pages * page_slots)
-    key_mask = usable[:, None, :]
-    row_max = jnp.max(jnp.where(key_mask, scores, -jnp.inf), axis=-1, keepdims=True)
-    weights = jnp.where(key_mask, jnp.exp(scores - row_max), 0.0)
-    denominator = jnp.sum(weights, axis=-1, keepdims=True)
-    rounded = weights.astype(jnp.bfloat16).reshape(req_count * group_count, pool_pages * page_slots)
-    mixed_values = jnp.dot(rounded, value_rows, preferred_element_type=jnp.float32).reshape(
-        req_count, group_count, head_dim
-    )
-    attended = (
-        (mixed_values / denominator).astype(jnp.bfloat16).reshape(req_count, group_count * head_dim)
-    )
-    stream = residual_in.astype(jnp.float32) + lax.psum_scatter(
-        jnp.dot(attended, w_out, preferred_element_type=jnp.float32),
-        "kvh",
-        scatter_dimension=0,
-        tiled=True,
-    )
-    inverse_rms = lax.rsqrt(jnp.mean(stream * stream, axis=-1, keepdims=True) + 1e-06)
-    normed = (stream * inverse_rms * norm_gain.astype(jnp.float32)).astype(jnp.bfloat16)
+    attended = attend(queries, key_cache, value_cache, lengths, page_table)
+    part = jnp.dot(attended, w_out, preferred_element_type=jnp.float32)
+    stream, normed = summed_stream(part, residual_in, norm_gain, lax.axis_size("kvh"))
     logit_max = jnp.max(route_logits, axis=-1, keepdims=True)
     logit_exp = jnp.exp(route_logits - logit_max)
     gate_weights = logit_exp / jnp.sum(logit_exp, axis=-1, keepdims=True)

time: 187 us -> 104 us (0.56)
  matrix products: 53.6 us -> 11.9 us
  other arithmetic: 28.6 us -> 4.39 us
  waiting for transfers between devices: 50 us -> 26.1 us
  between operations: 13.6 us -> 0.24 us
  Pallas kernels: 0 us -> 11.1 us
  local copies, waits for them, and re-layouts: 5.9 us -> 13.5 us
    dot_general x3, matrix products: 41.2 us -> 2.33 us  [the longest x1 1.19 us: attend(): jnp.einsum('rp,rx->px', spread, queries.reshape(req_count, group_count *...]
    reduce_scatter x1 -> x0, waiting for transfers between devices: 23.9 us -> none  [local(): lax.psum_scatter(jnp.dot(attended, w_out, preferred_element_type=jnp.floa...]
    reduce_sum x3 -> x2, other arithmetic: 21.7 us -> 0.89 us  [the longest x1 0.75 us: page_owners(): fill = jnp.sum(jnp.where(matched, counts[:, :, None], 0), axis=1)]
    pallas_call x0 -> x2, Pallas kernels: none -> 11.1 us  [the longest x1 6.49 us: summed_stream(): pl.pallas_call(functools.partial(sum_kernel, peers), in_specs=[vmem] * 3,...]
    unnamed x22 -> x29, local copies, waits for them, and re-layouts: 2.11 us -> 10.1 us
    and x1 -> x0, other arithmetic: 4.39 us -> none  [usable_slots(): usable = owned_page[:, :, None] & (position < lengths[:, None, None])]
    slice x0 -> x2, local copies, waits for them, and re-layouts: none -> 2.82 us  [attend(): top, total = (top[:, :, 0].T, total[:, :, 0].T)]
    and x1 -> x0, local copies, waits for them, and re-layouts: 1.95 us -> none  [usable_slots(): usable = owned_page[:, :, None] & (position < lengths[:, None, None])]
  transfers between devices with their start and end apart: 2 -> 1, of which waited for: 2 -> 1; matrix products, arithmetic and copies ran while one was open for 0% -> 0% of each run, Pallas kernels for 0% -> 0%
where the time goes in v1:
time: 104 us; the launch traced here: 103 us
  blocking collectives  32.3 us (31%)
  waiting for transfers between devices  26.1 us (25%)
  local copies, waits for them, and re-layouts  13.5 us (13%)
  matrix products  11.9 us (11%)
  Pallas kernels  11.1 us (11%)
  other arithmetic  4.39 us (4%)
  starting transfers between devices  3.75 us (4%)
    all_to_all x1, blocking collectives, local(): lax.all_to_all(outgoing, ('req', 'kvh'), split_axis=0, concat_axis=0, til...  32.3 us
    all_to_all x1, waiting for transfers between devices, local(): lax.all_to_all(produced.reshape(sources, width_slots, arrived_width), ('r...  26.1 us
    unnamed x29, local copies, waits for them, and re-layouts  10.1 us
    pallas_call x1, Pallas kernels, summed_stream(): pl.pallas_call(functools.partial(sum_kernel, peers), in_specs=[vmem] * 3,...  6.49 us
    dot_general x1, matrix products, local(): jnp.dot(hidden, w_down[0], preferred_element_type=jnp.float32)  5.52 us
    pallas_call x1, Pallas kernels, page_attention(): pl.pallas_call(functools.partial(page_kernel, head_dim ** (-0.5)), grid=(...  4.66 us
    all_to_all x1, starting transfers between devices, local(): lax.all_to_all(produced.reshape(sources, width_slots, arrived_width), ('r...  3.75 us
    slice x2, local copies, waits for them, and re-layouts, attend(): top, total = (top[:, :, 0].T, total[:, :, 0].T)  2.82 us
  transfers between devices with their start and end apart: 1, of which 1 were waited for; matrix products, arithmetic and copies ran while one was open for 0% of the time, Pallas kernels for 0%

profile of v1, /device:TPU:0, one launch (start us, length us, event | category | flops | bytes accessed | tf_op | source)
XLA Modules:
  0.0 103.3 jit_solution(12760717050311449494)
XLA Ops:
  0.0 0.9 copy.40
  1.0 0.7 subtract_clamp_fusion
  1.7 0.7 select_reduce_fusion.1
  2.5 1.2 %fusion.22 = bf16[20,8,8,128]{3,1,2,0:T(8,128)(2,1)S(1)} fusion(pred[64,160]{1,0:T(8,128)(4,1)S(1)} %broadcast_compare_fusion, bf16[8,8,8,128]{3,2,1,0:T(8,128)(2,1)} %bitcast.95), kind=kOutput, calls=%fused_computation.20 | convolution fusion | flops 21135360 | bytes 468992 | tf_op jit(solution)/shard_map/rp,rx->px/dot_general | solution.py:70
  3.7 0.2 broadcast_in_dim.89.filled_ref
  4.0 2.5 %copy-done.1 = bf16[160,1,128,128]{3,2,1,0:T(8,128)(2,1)S(1)} copy-done((bf16[160,1,128,128]{3,2,1,0:T(8,128)(2,1)S(1)}, bf16[160,1,128,128]{3,2,1,0:T(8,128)(2,1)}, u32[]{:S(2)}) %copy-start.1) | copy-done | bytes 5242904
  6.5 2.5 %copy-done.2 = bf16[160,1,128,128]{3,2,1,0:T(8,128)(2,1)S(1)} copy-done((bf16[160,1,128,128]{3,2,1,0:T(8,128)(2,1)S(1)}, bf16[160,1,128,128]{3,2,1,0:T(8,128)(2,1)}, u32[]{:S(2)}) %copy-start.2) | copy-done | bytes 5242904
  9.0 4.7 %shard_map.127 = (f32[160,8,128]{2,1,0:T(8,128)S(1)}, f32[160,8,128]{2,1,0:T(8,128)S(1)}, f32[160,8,128]{2,1,0:T(8,128)S(1)}) custom-call(s32[160,1,128]{2,1,0:T(1,128)S(1)} %broadcast_in_dim.89.filled_ref, bf16[160,8,128]{2,1,0:T(8,128)(2,1)S(1)} %bitcast.91, bf16[160,128,128]{2,1,0:T(8,128)(2,1)S(1)} %bitcast.89, bf16[160,128,128]{2,1,0:T(8,128)(2,1)S(1)} %bitcast.90), custom_call_target="tpu_custom_call" | custom-call | tf_op jit(solution)/shard_map/pallas_call | solution.py:55
  13.6 0.8 copy-done.3
  14.5 0.9 copy-done.4
  15.3 0.9 copy-done.5
  16.2 1.4 %copy.44 = f32[160,8,1]{0,1,2:T(8,128)S(1)} copy(f32[160,8,1]{2,1,0:T(8,128)} %bitcast.93) | data formatting | bytes 10240 | tf_op jit(solution)/shard_map/slice | solution.py:82
  17.6 1.4 %copy.41 = f32[160,8,1]{0,1,2:T(8,128)S(1)} copy(f32[160,8,1]{2,1,0:T(8,128)} %bitcast.92) | data formatting | bytes 10240 | tf_op jit(solution)/shard_map/slice | solution.py:82
  19.0 0.2 fusion.57
  19.2 0.1 select_reduce_fusion.3
  19.4 0.1 copy.42
  19.7 0.2 convert_reduce_fusion
  20.0 0.1 fusion.46
  20.1 1.5 %multiply_convert_fusion = (bf16[160,8,128]{2,1,0:T(8,128)(2,1)S(1)}, bf16[160,8,128]{2,1,0:T(8,128)(2,1)S(1)}) fusion(f32[160,8,128]{2,1,0:T(8,128)} %copy-done.3, f32[160,8]{1,0:T(8,128)S(1)} %copy.42), kind=kLoop, calls=%fused_computation.34 | loop fusion | flops 819200 | bytes 1315840 | tf_op jit(solution)/shard_map/convert_element_type | solution.py:88
  21.7 0.3 fusion.24
  22.0 0.4 copy-done.7
  22.4 0.8 fusion.41.part_ref
  23.2 6.5 %shard_map.128 = (f32[16,2048]{1,0:T(8,128)S(1)}, bf16[16,2048]{1,0:T(8,128)(2,1)S(1)}) custom-call(f32[64,2048]{1,0:T(8,128)S(1)} %fusion.41.part_ref, bf16[16,2048]{1,0:T(8,128)(2,1)S(1)} %copy-done.6, bf16[1,2048]{1,0:T(2,128)(2,1)S(1)} %reshape.142.gain_ref), custom_call_target="tpu_custom_call" | custom-call | tf_op jit(solution)/shard_map/pallas_call | solution.py:137
  29.7 0.5 fusion.13
  30.2 32.3 %all_to_all.10 = bf16[32,8,2048]{2,1,0:T(8,128)(2,1)S(1)} all-to-all(bf16[32,8,2048]{2,1,0:T(8,128)(2,1)S(1)} %fusion.13), channel_id=1, replica_groups=mesh['req'=8,'kvh'=4] {'req','kvh'}, dimensions={0} | all-to-all | bytes 2097152 | tf_op jit(solution)/shard_map/all_to_all | solution.py:199
  62.5 1.0 copy-done.8
  63.5 1.9 %fusion.5 = f32[256,768]{1,0:T(8,128)} fusion(bf16[1,2048,768]{2,1,0:T(8,128)(2,1)S(1)} %copy-done.12, bf16[32,8,2048]{2,1,0:T(8,128)(2,1)S(1)} %all_to_all.10), kind=kOutput, calls=%fused_computation.5 | convolution fusion | flops 805306368 | bytes 4980736 | tf_op jit(solution)/shard_map/dot_general | solution.py:202
  65.4 5.5 %fusion.10 = bf16[32,8,2048]{2,1,0:T(8,128)(2,1)} fusion(bf16[1,768,2048]{2,1,0:T(8,128)(2,1)S(1)} %copy-done, bf16[1,2048,768]{2,1,0:T(8,128)(2,1)} %param.24, bf16[32,8,2048]{2,1,0:T(8,128)(2,1)} %copy-done.8, f32[256,768]{1,0:T(8,128)} %fusion.5), kind=kOutput, calls=%fused_computation.11 | convolution fusion | flops 1612120064 | bytes 9175040 | tf_op jit(solution)/shard_map/dot_general | solution.py:205
  71.0 3.8 %all-to-all-start.1 = ((bf16[32,8,2048]{2,1,0:T(8,128)(2,1)}), bf16[32,8,2048]{2,1,0:T(8,128)(2,1)}, u32[]{:S(2)}, u32[]{:S(2)}) async-start(bf16[32,8,2048]{2,1,0:T(8,128)(2,1)} %fusion.10), calls=%async_computation.1 | async-start | bytes 2097152 | tf_op jit(solution)/shard_map/all_to_all | solution.py:206
  74.9 26.1 %all-to-all-done.1 = bf16[32,8,2048]{2,1,0:T(8,128)(2,1)} async-done(((bf16[32,8,2048]{2,1,0:T(8,128)(2,1)}), bf16[32,8,2048]{2,1,0:T(8,128)(2,1)}, u32[]{:S(2)}, u32[]{:S(2)}) %all-to-all-start.1) | async-done | bytes 1048608 | tf_op jit(solution)/shard_map/all_to_all | solution.py:206
  100.9 1.7 %fusion.20 = f32[16,2048]{1,0:T(8,128)S(1)} fusion(bf16[32,8,2048]{2,1,0:T(8,128)(2,1)} %all-to-all-done.1, f32[16,8]{1,0:T(8,128)S(1)} %copy.46, s32[16,8]{1,0:T(8,128)S(1)} %multiply_add_fusion), kind=kOutput, calls=%fused_computation.17 | convolution fusion | flops 134742016 | bytes 1180672 | tf_op jit(solution)/shard_map/dot_general | solution.py:215
  102.7 0.6 add_convert_fusion
  (34 shorter events, 0.6 us)
Async XLA Ops:
  0.0 65.4 %copy-start = (bf16[1,768,2048]{2,1,0:T(8,128)(2,1)S(1)}, bf16[1,768,2048]{2,1,0:T(8,128)(2,1)}, u32[]{:S(2)}) copy-start(bf16[1,768,2048]{2,1,0:T(8,128)(2,1)} %param.25) | copy-start | bytes 9437188
  4.0 2.5 %copy-start.1 = (bf16[160,1,128,128]{3,2,1,0:T(8,128)(2,1)S(1)}, bf16[160,1,128,128]{3,2,1,0:T(8,128)(2,1)}, u32[]{:S(2)}) copy-start(bf16[160,1,128,128]{3,2,1,0:T(8,128)(2,1)} %param.14) | copy-start | bytes 15728644
  6.5 2.5 %copy-start.2 = (bf16[160,1,128,128]{3,2,1,0:T(8,128)(2,1)S(1)}, bf16[160,1,128,128]{3,2,1,0:T(8,128)(2,1)}, u32[]{:S(2)}) copy-start(bf16[160,1,128,128]{3,2,1,0:T(8,128)(2,1)} %param.15) | copy-start | bytes 15728644
  8.9 10.5 %copy-start.10 = (bf16[2048]{0:T(1024)(128)(2,1)S(1)}, bf16[2048]{0:T(1024)(128)(2,1)}, u32[]{:S(2)}) copy-start(bf16[2048]{0:T(1024)(128)(2,1)} %param.20) | copy-start | bytes 12292
  8.9 10.6 %copy-start.11 = (s32[16,8]{0,1:T(8,128)S(1)}, s32[16,8]{0,1:T(8,128)}, u32[]{:S(2)}) copy-start(s32[16,8]{0,1:T(8,128)} %param.22) | copy-start | bytes 1540
  13.6 0.8 copy-start.3
  14.5 0.9 copy-start.4
  15.3 0.9 copy-start.5
  19.9 2.4 %copy-start.7 = (bf16[1024,2048]{1,0:T(8,128)(2,1)S(1)}, bf16[1024,2048]{1,0:T(8,128)(2,1)}, u32[]{:S(2)}) copy-start(bf16[1024,2048]{1,0:T(8,128)(2,1)} %param.19) | copy-start | bytes 12582916
  21.6 1.6 %copy-start.6 = (bf16[16,2048]{1,0:T(8,128)(2,1)S(1)}, bf16[16,2048]{1,0:T(8,128)(2,1)}, u32[]{:S(2)}) copy-start(bf16[16,2048]{1,0:T(8,128)(2,1)} %residual_ref.1) | copy-start | bytes 196612
  22.4 41.2 %copy-start.12 = (bf16[1,2048,768]{2,1,0:T(8,128)(2,1)S(1)}, bf16[1,2048,768]{2,1,0:T(8,128)(2,1)}, u32[]{:S(2)}) copy-start(bf16[1,2048,768]{2,1,0:T(8,128)(2,1)} %param.23) | copy-start | bytes 9437188
  62.5 1.0 %copy-start.8 = (bf16[32,8,2048]{2,1,0:T(8,128)(2,1)}, bf16[32,8,2048]{2,1,0:T(8,128)(2,1)S(1)}, u32[]{:S(2)}) copy-start(bf16[32,8,2048]{2,1,0:T(8,128)(2,1)S(1)} %all_to_all.10) | copy-start | bytes 3145732
  65.4 9.3 %copy-start.9 = (f32[16,8]{0,1:T(8,128)S(1)}, f32[16,8]{0,1:T(8,128)}, u32[]{:S(2)}) copy-start(f32[16,8]{0,1:T(8,128)} %param.21) | copy-start | bytes 1540
  71.0 30.0 %all-to-all-start.1 = ((bf16[32,8,2048]{2,1,0:T(8,128)(2,1)}), bf16[32,8,2048]{2,1,0:T(8,128)(2,1)}, u32[]{:S(2)}, u32[]{:S(2)}) async-start(bf16[32,8,2048]{2,1,0:T(8,128)(2,1)} %fusion.10), calls=%async_computation.1 | async-start | bytes 2097152 | tf_op jit(solution)/shard_map/all_to_all | solution.py:206

commit v2 on v1

--- a/solution.py
+++ b/solution.py
@@ -190,15 +190,19 @@
     pair_slots = earlier_count(pair_routes)
     target = pair_routes * slot_depth + pair_slots
     slot_ids = jnp.arange(expert_count * slot_depth, dtype=jnp.int32)
-    chosen = (target[None, :] == slot_ids[:, None]).reshape(
-        expert_count * slot_depth, token_count, pick_count
-    )
-    send_matrix = jnp.any(chosen, axis=-1).astype(jnp.bfloat16)
-    outgoing = jnp.dot(send_matrix, normed, preferred_element_type=jnp.float32).astype(jnp.bfloat16)
-    outgoing = outgoing.reshape(expert_count, slot_depth, model_width)
-    arrived = lax.all_to_all(outgoing, ("req", "kvh"), split_axis=0, concat_axis=0, tiled=True)
-    sources, width_slots, arrived_width = arrived.shape
-    flat_rows = arrived.reshape(sources * width_slots, arrived_width)
+    axes = ("req", "kvh")
+    all_routes = lax.all_gather(routes, axes, axis=0, tiled=True)
+    mine = lax.axis_index("req") * lax.axis_size("kvh") + lax.axis_index("kvh")
+    named = jnp.any(all_routes == mine, axis=-1).reshape(expert_count, token_count)
+    tokens = jnp.arange(token_count, dtype=jnp.int32)
+    earlier = named[:, None, :] & (tokens[None, None, :] < tokens[None, :, None])
+    rank = jnp.sum(earlier.astype(jnp.int32), axis=-1)
+    place = jnp.arange(expert_count, dtype=jnp.int32)[:, None] * slot_depth + rank
+    place = jnp.where(named, place, -1).reshape(expert_count * token_count)
+    take = (place[None, :] == slot_ids[:, None]).astype(jnp.bfloat16)
+    all_normed = lax.all_gather(normed, axes, axis=0, tiled=True)
+    flat_rows = jnp.dot(take, all_normed, preferred_element_type=jnp.float32).astype(jnp.bfloat16)
+    sources, width_slots, arrived_width = expert_count, slot_depth, model_width
     gate_part = jnp.dot(flat_rows, w_gate[0], preferred_element_type=jnp.float32)
     up_part = jnp.dot(flat_rows, w_up[0], preferred_element_type=jnp.float32)
     hidden = swish_gate(gate_part, up_part).astype(jnp.bfloat16)

time: 104 us -> 145 us (1.39)
  waiting for transfers between devices: 26.1 us -> 41.2 us
  between operations: 0.24 us -> 13.6 us
  blocking collectives: 32.3 us -> 42.2 us
  matrix products: 11.9 us -> 13.9 us
    all_gather x0 -> x1, blocking collectives: none -> 42.2 us  [local(): all_routes = lax.all_gather(routes, axes, axis=0, tiled=True)]
    all_to_all x1 -> x0, blocking collectives: 32.3 us -> none  [local(): lax.all_to_all(outgoing, ('req', 'kvh'), split_axis=0, concat_axis=0, til...]
    all_gather x0 -> x1, waiting for transfers between devices: none -> 15.6 us  [local(): all_normed = lax.all_gather(normed, axes, axis=0, tiled=True)]
    dot_general x1, matrix products: 0.47 us -> 2.46 us  [local(): jnp.dot(take, all_normed, preferred_element_type=jnp.float32)]
  transfers between devices with their start and end apart: 1 -> 2, of which waited for: 1 -> 2; matrix products, arithmetic and copies ran while one was open for 0% -> 1% of each run, Pallas kernels for 0% -> 0%
where the time goes in v2:
time: 145 us
  blocking collectives  42.2 us (29%)
  waiting for transfers between devices  41.2 us (28%)
  matrix products  13.9 us (10%)
  local copies, waits for them, and re-layouts  13.8 us (10%)
  between operations  13.6 us (9%)
  Pallas kernels  11.8 us (8%)
  other arithmetic  4.53 us (3%)
  starting transfers between devices  3.59 us (2%)
    all_gather x1, blocking collectives, local(): all_routes = lax.all_gather(routes, axes, axis=0, tiled=True)  42.2 us
    all_to_all x1, waiting for transfers between devices, local(): lax.all_to_all(produced.reshape(sources, width_slots, arrived_width), ('r...  25.6 us
    all_gather x1, waiting for transfers between devices, local(): all_normed = lax.all_gather(normed, axes, axis=0, tiled=True)  15.6 us
    unnamed x29, local copies, waits for them, and re-layouts  10.2 us
    pallas_call x1, Pallas kernels, summed_stream(): pl.pallas_call(functools.partial(sum_kernel, peers), in_specs=[vmem] * 3,...  7.1 us
    dot_general x1, matrix products, local(): jnp.dot(hidden, w_down[0], preferred_element_type=jnp.float32)  5.52 us
    pallas_call x1, Pallas kernels, page_attention(): pl.pallas_call(functools.partial(page_kernel, head_dim ** (-0.5)), grid=(...  4.66 us
    all_to_all x1, starting transfers between devices, local(): lax.all_to_all(produced.reshape(sources, width_slots, arrived_width), ('r...  3.58 us
  transfers between devices with their start and end apart: 2, of which 2 were waited for; matrix products, arithmetic and copies ran while one was open for 1% of the time, Pallas kernels for 0%

profile of v2, /device:TPU:0, one launch (start us, length us, event | category | flops | bytes accessed | tf_op | source)
XLA Modules:
  0.0 144.7 jit_solution(16383551441272441777)
XLA Ops:
  6.5 0.9 copy.59
  7.5 0.7 subtract_clamp_fusion
  8.2 0.7 select_reduce_fusion.1
  9.0 1.2 fusion.21
  10.3 0.2 broadcast_in_dim.95.filled_ref
  10.5 2.5 %copy-done.1 = bf16[160,1,128,128]{3,2,1,0:T(8,128)(2,1)S(1)} copy-done((bf16[160,1,128,128]{3,2,1,0:T(8,128)(2,1)S(1)}, bf16[160,1,128,128]{3,2,1,0:T(8,128)(2,1)}, u32[]{:S(2)}) %copy-start.1) | copy-done | bytes 5242904
  13.0 2.5 %copy-done.2 = bf16[160,1,128,128]{3,2,1,0:T(8,128)(2,1)S(1)} copy-done((bf16[160,1,128,128]{3,2,1,0:T(8,128)(2,1)S(1)}, bf16[160,1,128,128]{3,2,1,0:T(8,128)(2,1)}, u32[]{:S(2)}) %copy-start.2) | copy-done | bytes 5242904
  15.5 4.7 %shard_map.127 = (f32[160,8,128]{2,1,0:T(8,128)S(1)}, f32[160,8,128]{2,1,0:T(8,128)S(1)}, f32[160,8,128]{2,1,0:T(8,128)S(1)}) custom-call(s32[160,1,128]{2,1,0:T(1,128)S(1)} %broadcast_in_dim.95.filled_ref, bf16[160,8,128]{2,1,0:T(8,128)(2,1)S(1)} %bitcast.84, bf16[160,128,128]{2,1,0:T(8,128)(2,1)S(1)} %bitcast.82, bf16[160,128,128]{2,1,0:T(8,128)(2,1)S(1)} %bitcast.83), custom_call_target="tpu_custom_call" | custom-call | tf_op jit(solution)/shard_map/pallas_call | solution.py:55
  20.1 0.8 copy-done.3
  21.0 0.9 copy-done.4
  21.8 0.9 copy-done.5
  22.7 1.4 copy.63
  24.1 1.4 copy.60
  25.5 0.2 fusion.52
  25.8 0.1 select_reduce_fusion.3
  26.1 1.5 %multiply_convert_fusion = (bf16[160,8,128]{2,1,0:T(8,128)(2,1)S(1)}, bf16[160,8,128]{2,1,0:T(8,128)(2,1)S(1)}) fusion(f32[160,8,128]{2,1,0:T(8,128)} %copy-done.3, f32[160,8]{1,0:T(8,128)S(1)} %copy.61), kind=kLoop, calls=%fused_computation.31 | loop fusion | flops 819200 | bytes 1315840 | tf_op jit(solution)/shard_map/convert_element_type | solution.py:88
  27.6 0.3 fusion.23
  27.9 0.5 copy-done.7
  28.4 0.9 fusion.37.part_ref
  29.3 7.1 %shard_map.128 = (f32[16,2048]{1,0:T(8,128)S(1)}, bf16[16,2048]{1,0:T(8,128)(2,1)}) custom-call(f32[64,2048]{1,0:T(8,128)S(1)} %fusion.37.part_ref, bf16[16,2048]{1,0:T(8,128)(2,1)S(1)} %copy-done.6, bf16[1,2048]{1,0:T(2,128)(2,1)S(1)} %reshape.156.gain_ref), custom_call_target="tpu_custom_call" | custom-call | tf_op jit(solution)/shard_map/pallas_call | solution.py:137
  36.4 42.2 %all-gather = s32[32,16,8]{1,2,0:T(8,128)S(1)} all-gather(s32[1,16,8]{1,2,0:T(8,128)S(1)} %bitcast.90), channel_id=1, replica_groups=mesh['req'=8,'kvh'=4] {'req','kvh'}, dimensions={0}, use_global_device_ids=true | all-gather | bytes 16896 | tf_op jit(solution)/shard_map/all_gather | solution.py:194
  78.8 0.1 convert_reduce_fusion
  79.2 15.6 %all-gather.3.cloned.1.call-done = bf16[512,2048]{1,0:T(8,128)(2,1)} async-done(((bf16[16,2048]{1,0:T(8,128)(2,1)}), bf16[512,2048]{1,0:T(8,128)(2,1)}) %all-gather.3.cloned.1.call-update) | async-done | bytes 2097168 | tf_op jit(solution)/shard_map/all_gather | solution.py:203
  94.7 2.5 %convolution_convert_fusion = bf16[256,2048]{1,0:T(8,128)(2,1)S(1)} fusion(bf16[512,2048]{1,0:T(8,128)(2,1)} %all-gather.3.cloned.1.call-done, s32[512]{0:T(512)S(1)} %reshape.166), kind=kOutput, calls=%fused_computation.9 | convolution fusion | flops 537526272 | bytes 3147776 | tf_op jit(solution)/shard_map/dot_general | solution.py:204
  97.2 1.0 copy-done.8
  98.2 1.9 %fusion.5 = f32[256,768]{1,0:T(8,128)} fusion(bf16[256,2048]{1,0:T(8,128)(2,1)S(1)} %convolution_convert_fusion, bf16[1,2048,768]{2,1,0:T(8,128)(2,1)S(1)} %copy-done.12), kind=kOutput, calls=%fused_computation.5 | convolution fusion | flops 805306368 | bytes 4980736 | tf_op jit(solution)/shard_map/dot_general | solution.py:206
  100.1 5.5 %fusion.10 = bf16[32,8,2048]{2,1,0:T(8,128)(2,1)} fusion(bf16[1,768,2048]{2,1,0:T(8,128)(2,1)S(1)} %copy-done, bf16[256,2048]{1,0:T(8,128)(2,1)} %copy-done.8, bf16[1,2048,768]{2,1,0:T(8,128)(2,1)} %param.24, f32[256,768]{1,0:T(8,128)} %fusion.5), kind=kOutput, calls=%fused_computation.11 | convolution fusion | flops 1612120064 | bytes 9175040 | tf_op jit(solution)/shard_map/dot_general | solution.py:209
  105.7 3.6 %all-to-all-start = ((bf16[32,8,2048]{2,1,0:T(8,128)(2,1)}), bf16[32,8,2048]{2,1,0:T(8,128)(2,1)}, u32[]{:S(2)}, u32[]{:S(2)}) async-start(bf16[32,8,2048]{2,1,0:T(8,128)(2,1)} %fusion.10), calls=%async_computation | async-start | bytes 2097152 | tf_op jit(solution)/shard_map/all_to_all | solution.py:210
  109.5 0.2 convert_reduce_fusion.1
  109.8 25.6 %all-to-all-done = bf16[32,8,2048]{2,1,0:T(8,128)(2,1)} async-done(((bf16[32,8,2048]{2,1,0:T(8,128)(2,1)}), bf16[32,8,2048]{2,1,0:T(8,128)(2,1)}, u32[]{:S(2)}, u32[]{:S(2)}) %all-to-all-start) | async-done | bytes 1048608 | tf_op jit(solution)/shard_map/all_to_all | solution.py:210
  135.5 1.7 %fusion.19 = f32[16,2048]{1,0:T(8,128)S(1)} fusion(bf16[32,8,2048]{2,1,0:T(8,128)(2,1)} %all-to-all-done, f32[16,8]{1,0:T(8,128)S(1)} %copy.65, s32[16,8]{1,0:T(8,128)S(1)} %multiply_add_fusion), kind=kOutput, calls=%fused_computation.16 | convolution fusion | flops 134742016 | bytes 1180672 | tf_op jit(solution)/shard_map/dot_general | solution.py:219
  137.2 0.6 add_convert_fusion
  (44 shorter events, 1.1 us)
Async XLA Ops:
  6.5 93.6 %copy-start = (bf16[1,768,2048]{2,1,0:T(8,128)(2,1)S(1)}, bf16[1,768,2048]{2,1,0:T(8,128)(2,1)}, u32[]{:S(2)}) copy-start(bf16[1,768,2048]{2,1,0:T(8,128)(2,1)} %param.25) | copy-start | bytes 9437188
  6.5 88.2 %all-gather.3.cloned.1.call-start = ((), (), s32[]{:S(2)}) async-start(), calls=%async_computation.1 | async-start | bytes 2162688 | tf_op jit(solution)/shard_map/all_gather | solution.py:203
  10.5 2.5 %copy-start.1 = (bf16[160,1,128,128]{3,2,1,0:T(8,128)(2,1)S(1)}, bf16[160,1,128,128]{3,2,1,0:T(8,128)(2,1)}, u32[]{:S(2)}) copy-start(bf16[160,1,128,128]{3,2,1,0:T(8,128)(2,1)} %param.14) | copy-start | bytes 15728644
  13.0 2.5 %copy-start.2 = (bf16[160,1,128,128]{3,2,1,0:T(8,128)(2,1)S(1)}, bf16[160,1,128,128]{3,2,1,0:T(8,128)(2,1)}, u32[]{:S(2)}) copy-start(bf16[160,1,128,128]{3,2,1,0:T(8,128)(2,1)} %param.15) | copy-start | bytes 15728644
  15.5 10.5 %copy-start.11 = (bf16[2048]{0:T(1024)(128)(2,1)S(1)}, bf16[2048]{0:T(1024)(128)(2,1)}, u32[]{:S(2)}) copy-start(bf16[2048]{0:T(1024)(128)(2,1)} %param.20) | copy-start | bytes 12292
  20.1 0.8 copy-start.3
  21.0 0.9 copy-start.4
  21.8 0.9 copy-start.5
  26.0 2.4 %copy-start.7 = (bf16[1024,2048]{1,0:T(8,128)(2,1)S(1)}, bf16[1024,2048]{1,0:T(8,128)(2,1)}, u32[]{:S(2)}) copy-start(bf16[1024,2048]{1,0:T(8,128)(2,1)} %param.19) | copy-start | bytes 12582916
  27.6 1.7 %copy-start.6 = (bf16[16,2048]{1,0:T(8,128)(2,1)S(1)}, bf16[16,2048]{1,0:T(8,128)(2,1)}, u32[]{:S(2)}) copy-start(bf16[16,2048]{1,0:T(8,128)(2,1)} %residual_ref.1) | copy-start | bytes 196612
  28.4 8.0 %copy-start.10 = (s32[16,8]{0,1:T(8,128)S(1)}, s32[16,8]{0,1:T(8,128)}, u32[]{:S(2)}) copy-start(s32[16,8]{0,1:T(8,128)} %param.22) | copy-start | bytes 1540
  94.7 3.5 %copy-start.12 = (bf16[1,2048,768]{2,1,0:T(8,128)(2,1)S(1)}, bf16[1,2048,768]{2,1,0:T(8,128)(2,1)}, u32[]{:S(2)}) copy-start(bf16[1,2048,768]{2,1,0:T(8,128)(2,1)} %param.23) | copy-start | bytes 9437188
  97.2 1.0 copy-start.8
  100.1 9.2 %copy-start.9 = (f32[16,8]{0,1:T(8,128)S(1)}, f32[16,8]{0,1:T(8,128)}, u32[]{:S(2)}) copy-start(f32[16,8]{0,1:T(8,128)} %param.21) | copy-start | bytes 1540
  105.7 29.8 %all-to-all-start = ((bf16[32,8,2048]{2,1,0:T(8,128)(2,1)}), bf16[32,8,2048]{2,1,0:T(8,128)(2,1)}, u32[]{:S(2)}, u32[]{:S(2)}) async-start(bf16[32,8,2048]{2,1,0:T(8,128)(2,1)} %fusion.10), calls=%async_computation | async-start | bytes 2097152 | tf_op jit(solution)/shard_map/all_to_all | solution.py:210
Sparse Core Ops, SparseCore 0:
  36.5 58.1 all-gather.2
